TPU v7x, 256 devices: a whole 4x4x8 slice. The times are simulated.
256 devices in a mesh: ops: 32 (over y, x, core), sec: 8 (over z).
Axes of the slice: x: 4, y: 4, z: 8, core: 2. Of those that a mesh axis runs over, the one named last changes fastest.
Arguments:
- left_ops: bfloat16 [128, 16, 256, 256], P('ops', 'sec'), as said below
- right_ops: bfloat16 [128, 16, 256, 256], P('ops', 'sec'), as said below
- pattern: int32 [128, 16], P('ops', 'sec'), may hold values from 0 to 1, as said below
- guess_vector: float32 [16, 256, 256], P('sec'), may hold values from -6 to 6
- precond: float32 [16, 256, 256], P('sec'), may hold values from 0.5 to 8
- rotation: bfloat16 [16, 256, 256], P('sec', None, 'ops'), may hold values from -1.5 to 1.5
Outputs:
- new_state: float32 [16, 256, 256], P('sec', 'ops')
- energy: float32 [1], replicated
- renormalized: bfloat16 [128, 16, 256, 256], P('ops', 'sec')
Inputs may be any that keep to these rules, and one draw needn't show every extreme that they name: pattern[k, s] is 1 where operator k has a block in sector s, else 0. Every block left_ops[k, s] is symmetric. Every block right_ops[k, s] is symmetric.
All inputs are finite; a program needn't handle non-finite values.
Results may differ from a plain program's by a relative error of at most 0.009.
Values may be sent and summed in bfloat16 or wider, within the bound.
No kernel may reach another device: no remote copies, remote signals or barrier semaphores. Data moves between devices by JAX's collectives and lax.ppermute only.
A program may use at most 64 MiB of HBM per device.

v0:
```python
import jax
import jax.numpy as jnp
from jax import lax
from jax.sharding import PartitionSpec as P


def local_sigma(vector, left_ops, right_ops, pattern):
    vec_low = vector.astype(jnp.bfloat16)
    halfway = jnp.einsum(
        "ksij,sjl->ksil", left_ops, vec_low, preferred_element_type=jnp.float32
    ).astype(jnp.bfloat16)
    halfway = halfway * pattern.astype(jnp.bfloat16)[:, :, None, None]
    return jnp.einsum("ksil,ksml->sim", halfway, right_ops, preferred_element_type=jnp.float32)


def local(left_ops, right_ops, pattern, guess_vector, precond, rotation):
    sector_count = guess_vector.shape[0]
    states = guess_vector.shape[1]
    row_count = states // lax.axis_size("ops")
    row_start = lax.axis_index("ops") * row_count
    entries = float(sector_count * lax.axis_size("sec") * states * states)

    def owned(array):
        return lax.dynamic_slice_in_dim(array, row_start, row_count, 1)

    rotate_full = lax.all_gather(rotation, "ops", axis=2, tiled=True)
    rotated = jnp.einsum(
        "ksij,sjl->ksil", left_ops, rotate_full, preferred_element_type=jnp.float32
    ).astype(jnp.bfloat16)
    renormalized = jnp.einsum(
        "sji,ksjl->ksil", rotate_full, rotated, preferred_element_type=jnp.float32
    ).astype(jnp.bfloat16)
    guess_rows = owned(guess_vector)
    guess_sum = lax.psum(jnp.sum(guess_rows * guess_rows), ("ops", "sec"))
    first_full = guess_vector * (1.0 / jnp.sqrt(guess_sum / entries + 1e-06))

    def apply_whole(vector):
        return lax.psum(local_sigma(vector, left_ops, right_ops, pattern), "ops")

    def local_part(array):
        return owned(array)

    def local_product(left, right):
        return jnp.sum(local_part(left) * local_part(right))

    image_first = apply_whole(first_full)
    rayleigh_first = lax.psum(local_product(first_full, image_first), ("ops", "sec")) / entries
    correction = (image_first - rayleigh_first * first_full) / precond
    correlation = lax.psum(local_product(first_full, correction), ("ops", "sec")) / entries
    orthogonal = correction - correlation * first_full
    orth_square = lax.psum(local_product(orthogonal, orthogonal), ("ops", "sec")) / entries
    second = orthogonal * (1.0 / jnp.sqrt(orth_square + 1e-06))
    image_second = apply_whole(second)
    coupling_sum, second_sum = lax.psum(
        (local_product(first_full, image_second), local_product(second, image_second)),
        ("ops", "sec"),
    )
    coupling = coupling_sum / entries
    rayleigh_second = second_sum / entries
    half_gap = (rayleigh_first - rayleigh_second) / 2
    energy = (rayleigh_first + rayleigh_second) / 2 - jnp.sqrt(
        half_gap * half_gap + coupling * coupling
    )
    weight_first = rayleigh_second - energy
    weight_second = -coupling
    scaling = jnp.sqrt(weight_first * weight_first + weight_second * weight_second)
    combined = (weight_first * first_full + weight_second * second) / scaling
    new_state = local_part(combined)
    return (new_state, jnp.reshape(energy, (1,)), renormalized)


def solution(mesh):
    return jax.shard_map(
        local,
        mesh=mesh,
        in_specs=(
            P("ops", "sec", None, None),
            P("ops", "sec", None, None),
            P("ops", "sec"),
            P("sec", None, None),
            P("sec", None, None),
            P("sec", None, "ops"),
        ),
        out_specs=(P("sec", "ops", None), P(), P("ops", "sec", None, None)),
        check_vma=False,
    )
```

profile of v0, /device:TPU:1, one launch (start us, length us, event | category | flops | bytes accessed | tf_op | source)
XLA Modules:
  0.0 659.4 jit_solution(3782549998908427796)
XLA Ops:
  7.2 0.0 copy-start
  7.2 0.0 copy-start.4
  7.2 0.0 all-reduce.4.cloned.1.call-start
  7.2 1.4 multiply_reduce_fusion.5
  8.6 81.4 %psum.56 = f32[]{:T(128)} all-reduce(f32[]{:T(128)} %multiply_reduce_fusion.5), channel_id=1, replica_groups=mesh['ops'=32,'sec'=8] {'ops','sec'}, use_global_device_ids=true, to_apply=%region_1.0 | all-reduce | flops 1 | bytes 8 | tf_op jit(solution)/shard_map/psum | solution.py:34
  90.7 1.1 broadcast_multiply_fusion.1
  91.8 0.0 copy-done.4
  91.8 0.0 copy-done
  91.8 0.0 copy-start.1
  91.8 0.0 copy-start.2
  91.9 2.8 fusion.8
  94.7 0.0 all-reduce.4.cloned.1.call-update
  94.7 0.0 all-reduce.6.cloned.1.call-start
  94.8 108.9 %all-reduce.4.cloned.1.call-done = f32[2,256,256]{2,1,0:T(8,128)} async-done(((f32[2,256,256]{2,1,0:T(8,128)}), f32[2,256,256]{2,1,0:T(8,128)}) %all-reduce.4.cloned.1.call-update) | async-done | bytes 524304 | tf_op jit(solution)/shard_map/psum | solution.py:38
  203.6 1.3 multiply_reduce_fusion.4
  205.0 76.8 %psum.58 = f32[]{:T(128)} all-reduce(f32[]{:T(128)} %multiply_reduce_fusion.4), channel_id=1, replica_groups=mesh['ops'=32,'sec'=8] {'ops','sec'}, use_global_device_ids=true, to_apply=%region_4.0 | all-reduce | flops 1 | bytes 8 | tf_op jit(solution)/shard_map/psum | solution.py:47
  282.5 1.1 subtract_divide_fusion
  283.6 0.0 copy-start.3
  283.6 0.6 multiply_reduce_fusion.3
  284.2 73.4 %psum.59 = f32[]{:T(128)} all-reduce(f32[]{:T(128)} %multiply_reduce_fusion.3), channel_id=1, replica_groups=mesh['ops'=32,'sec'=8] {'ops','sec'}, use_global_device_ids=true, to_apply=%region_6.0 | all-reduce | flops 1 | bytes 8 | tf_op jit(solution)/shard_map/psum | solution.py:49
  358.3 0.1 multiply_subtract_fusion
  358.5 0.6 multiply_reduce_fusion.2
  359.1 24.0 %all_gather.3 = bf16[2,256,256]{1,2,0:T(8,128)(2,1)S(1)} all-gather(bf16[2,256,8]{1,2,0:T(8,128)(2,1)S(1)} %copy-done.3), channel_id=1, replica_groups=mesh['ops'=32,'sec'=8] {'ops'}, dimensions={2}, use_global_device_ids=true | all-gather | bytes 270336 | tf_op jit(solution)/shard_map/all_gather | solution.py:26
  383.0 73.3 %psum.60 = f32[]{:T(128)} all-reduce(f32[]{:T(128)} %multiply_reduce_fusion.2), channel_id=1, replica_groups=mesh['ops'=32,'sec'=8] {'ops','sec'}, use_global_device_ids=true, to_apply=%region_8.0 | all-reduce | flops 1 | bytes 8 | tf_op jit(solution)/shard_map/psum | solution.py:51
  457.1 2.8 fusion.9
  459.9 0.0 all-reduce.6.cloned.1.call-update
  459.9 0.7 fusion.3
  460.6 1.3 copy.11
  461.9 108.0 %all-reduce.6.cloned.1.call-done = f32[2,256,256]{2,1,0:T(8,128)} async-done(((f32[2,256,256]{2,1,0:T(8,128)}), f32[2,256,256]{2,1,0:T(8,128)}) %all-reduce.6.cloned.1.call-update) | async-done | bytes 524304 | tf_op jit(solution)/shard_map/psum | solution.py:38
  569.9 1.3 multiply_reduce_fusion
  571.2 76.9 %all-reduce = (f32[]{:T(128)}, f32[]{:T(128)}) all-reduce(f32[]{:T(128)} %get-tuple-element.7, f32[]{:T(128)} %get-tuple-element.6), channel_id=1, replica_groups=mesh['ops'=32,'sec'=8] {'ops','sec'}, use_global_device_ids=true, to_apply=%region_11.0 | all-reduce | flops 2 | bytes 16 | tf_op jit(solution)/shard_map/psum | solution.py:54
  650.8 0.6 add_divide_fusion
  (5 shorter events, 0.0 us)
Async XLA Ops:
  7.2 84.7 %copy-start = (bf16[4,2,256,256]{3,2,1,0:T(8,128)(2,1)S(1)}, bf16[4,2,256,256]{3,2,1,0:T(8,128)(2,1)}, u32[]{:S(2)}) copy-start(bf16[4,2,256,256]{3,2,1,0:T(8,128)(2,1)} %param.6) | copy-start | bytes 3145732
  7.2 84.6 %copy-start.4 = (s32[4,2]{0,1:T(2,128)S(1)}, s32[4,2]{0,1:T(2,128)}, u32[]{:S(2)}) copy-start(s32[4,2]{0,1:T(2,128)} %param.8) | copy-start | bytes 100
  7.2 196.4 %all-reduce.4.cloned.1.call-start = ((), (), s32[]{:S(2)}) async-start(), calls=%async_computation | async-start | bytes 1048576 | tf_op jit(solution)/shard_map/psum | solution.py:38
  91.8 190.6 %copy-start.1 = (f32[2,256,256]{2,1,0:T(8,128)S(1)}, f32[2,256,256]{2,1,0:T(8,128)}, u32[]{:S(2)}) copy-start(f32[2,256,256]{2,1,0:T(8,128)} %param.9) | copy-start | bytes 1572868
  91.8 190.6 %copy-start.2 = (f32[2,256,256]{2,1,0:T(8,128)S(1)}, f32[2,256,256]{2,1,0:T(8,128)}, u32[]{:S(2)}) copy-start(f32[2,256,256]{2,1,0:T(8,128)} %param.10) | copy-start | bytes 1572868
  94.7 475.2 %all-reduce.6.cloned.1.call-start = ((), (), s32[]{:S(2)}) async-start(), calls=%async_computation.1 | async-start | bytes 1048576 | tf_op jit(solution)/shard_map/psum | solution.py:38
  283.6 75.4 %copy-start.3 = (bf16[2,256,8]{1,2,0:T(8,128)(2,1)S(1)}, bf16[2,256,8]{1,2,0:T(8,128)(2,1)}, u32[]{:S(2)}) copy-start(bf16[2,256,8]{1,2,0:T(8,128)(2,1)} %param.11) | copy-start | bytes 24580
Sparse Core Ops, SparseCore 0:
  94.8 108.7 all-reduce.3
  460.0 109.8 all-reduce.5
where the time goes:
time: 661 us; the launch traced here: 659 us
  blocking collectives  406 us (61%)
  waiting for transfers between devices  217 us (33%)
  between operations  20.7 us (3%)
  other arithmetic  8.28 us (1%)
    psum x2, waiting for transfers between devices, apply_whole(): return lax.psum(local_sigma(vector, left_ops, right_ops, pattern), 'ops')  217 us
    psum x1, blocking collectives, local(): guess_sum = lax.psum(jnp.sum(guess_rows * guess_rows), ('ops', 'sec'))  81.4 us
    psum x1, blocking collectives, local(): lax.psum((local_product(first_full, image_second), local_product(second,...  76.9 us
    psum x1, blocking collectives, local(): lax.psum(local_product(first_full, image_first), ('ops', 'sec')) / entries  76.8 us
    psum x1, blocking collectives, local(): lax.psum(local_product(first_full, correction), ('ops', 'sec')) / entries  73.4 us
    psum x1, blocking collectives, local(): lax.psum(local_product(orthogonal, orthogonal), ('ops', 'sec')) / entries  73.3 us
    all_gather x1, blocking collectives, local(): rotate_full = lax.all_gather(rotation, 'ops', axis=2, tiled=True)  24 us
  transfers between devices with their start and end apart: 2, of which 2 were waited for; matrix products, arithmetic and copies ran while one was open for 0% of the time, Pallas kernels for 0%

commit v1 on v0

--- a/solution.py
+++ b/solution.py
@@ -44,7 +44,9 @@
         return jnp.sum(local_part(left) * local_part(right))
 
     image_first = apply_whole(first_full)
-    rayleigh_first = lax.psum(local_product(first_full, image_first), ("ops", "sec")) / entries
+    rayleigh_first = (
+        lax.psum(lax.psum(local_product(first_full, image_first), "sec"), "ops") / entries
+    )
     correction = (image_first - rayleigh_first * first_full) / precond
     correlation = lax.psum(local_product(first_full, correction), ("ops", "sec")) / entries
     orthogonal = correction - correlation * first_full

time: 661 us -> 664 us (level)
    psum x1 -> x2, blocking collectives: 76.8 us -> 81.5 us  [the longest x1 67.2 us: local(): lax.psum(lax.psum(local_product(first_full, image_first), 'sec'), 'ops')]
where the time goes in v1:
time: 664 us; the launch traced here: 663 us
  blocking collectives  410 us (62%)
  waiting for transfers between devices  216 us (33%)
  between operations  20.7 us (3%)
  other arithmetic  8.28 us (1%)
    psum x2, waiting for transfers between devices, apply_whole(): return lax.psum(local_sigma(vector, left_ops, right_ops, pattern), 'ops')  216 us
    psum x1, blocking collectives, local(): guess_sum = lax.psum(jnp.sum(guess_rows * guess_rows), ('ops', 'sec'))  81.4 us
    psum x1, blocking collectives, local(): lax.psum((local_product(first_full, image_second), local_product(second,...  76.9 us
    psum x1, blocking collectives, local(): lax.psum(local_product(orthogonal, orthogonal), ('ops', 'sec')) / entries  74.1 us
    psum x1, blocking collectives, local(): lax.psum(local_product(first_full, correction), ('ops', 'sec')) / entries  72.6 us
    psum x1, blocking collectives, local(): lax.psum(lax.psum(local_product(first_full, image_first), 'sec'), 'ops')  67.2 us
    all_gather x1, blocking collectives, local(): rotate_full = lax.all_gather(rotation, 'ops', axis=2, tiled=True)  23.4 us
    psum x1, blocking collectives, local(): lax.psum(local_product(first_full, image_first), 'sec')  14.3 us
  transfers between devices with their start and end apart: 2, of which 2 were waited for; matrix products, arithmetic and copies ran while one was open for 0% of the time, Pallas kernels for 0%

profile of v1, /device:TPU:1, one launch (start us, length us, event | category | flops | bytes accessed | tf_op | source)
XLA Modules:
  0.0 662.7 jit_solution(16715909615999951596)
XLA Ops:
  7.2 0.0 copy-start
  7.2 0.0 all-reduce.4.cloned.1.call-start
  7.2 1.4 multiply_reduce_fusion.5
  8.6 81.4 %psum.63 = f32[]{:T(128)} all-reduce(f32[]{:T(128)} %multiply_reduce_fusion.5), channel_id=1, replica_groups=mesh['ops'=32,'sec'=8] {'ops','sec'}, use_global_device_ids=true, to_apply=%region_1.0 | all-reduce | flops 1 | bytes 8 | tf_op jit(solution)/shard_map/psum | solution.py:34
  90.7 1.1 broadcast_multiply_fusion.1
  91.8 0.0 copy-start.1
  91.8 0.0 copy-start.2
  91.9 2.8 fusion.8
  94.7 0.0 all-reduce.4.cloned.1.call-update
  94.7 0.0 all-reduce.6.cloned.1.call-start
  94.8 108.9 %all-reduce.4.cloned.1.call-done = f32[2,256,256]{2,1,0:T(8,128)} async-done(((f32[2,256,256]{2,1,0:T(8,128)}), f32[2,256,256]{2,1,0:T(8,128)}) %all-reduce.4.cloned.1.call-update) | async-done | bytes 524304 | tf_op jit(solution)/shard_map/psum | solution.py:38
  203.6 1.3 multiply_reduce_fusion.4
  205.0 14.3 %psum.65 = f32[]{:T(128)} all-reduce(f32[]{:T(128)} %multiply_reduce_fusion.4), channel_id=1, replica_groups=mesh['ops'=32,'sec'=8] {'sec'}, use_global_device_ids=true, to_apply=%region_4.0 | all-reduce | flops 1 | bytes 8 | tf_op jit(solution)/shard_map/psum | solution.py:48
  219.3 67.2 %psum.66 = f32[]{:T(128)} all-reduce(f32[]{:T(128)} %psum.65), channel_id=1, replica_groups=mesh['ops'=32,'sec'=8] {'ops'}, use_global_device_ids=true, to_apply=%region_5.0 | all-reduce | flops 1 | bytes 8 | tf_op jit(solution)/shard_map/psum | solution.py:48
  287.1 0.0 copy-done.1
  287.1 0.0 copy-done.2
  287.1 1.1 subtract_divide_fusion
  288.3 0.0 copy-start.3
  288.3 0.6 multiply_reduce_fusion.3
  288.9 72.6 %psum.67 = f32[]{:T(128)} all-reduce(f32[]{:T(128)} %multiply_reduce_fusion.3), channel_id=1, replica_groups=mesh['ops'=32,'sec'=8] {'ops','sec'}, use_global_device_ids=true, to_apply=%region_7.0 | all-reduce | flops 1 | bytes 8 | tf_op jit(solution)/shard_map/psum | solution.py:51
  362.2 0.1 multiply_subtract_fusion
  362.3 0.6 multiply_reduce_fusion.2
  362.9 23.4 %all_gather.3 = bf16[2,256,256]{1,2,0:T(8,128)(2,1)S(1)} all-gather(bf16[2,256,8]{1,2,0:T(8,128)(2,1)S(1)} %copy-done.3), channel_id=1, replica_groups=mesh['ops'=32,'sec'=8] {'ops'}, dimensions={2}, use_global_device_ids=true | all-gather | bytes 270336 | tf_op jit(solution)/shard_map/all_gather | solution.py:26
  386.2 74.1 %psum.68 = f32[]{:T(128)} all-reduce(f32[]{:T(128)} %multiply_reduce_fusion.2), channel_id=1, replica_groups=mesh['ops'=32,'sec'=8] {'ops','sec'}, use_global_device_ids=true, to_apply=%region_9.0 | all-reduce | flops 1 | bytes 8 | tf_op jit(solution)/shard_map/psum | solution.py:53
  461.1 2.8 fusion.9
  463.9 0.0 all-reduce.6.cloned.1.call-update
  463.9 0.7 fusion.3
  464.7 1.3 copy.11
  466.0 107.2 %all-reduce.6.cloned.1.call-done = f32[2,256,256]{2,1,0:T(8,128)} async-done(((f32[2,256,256]{2,1,0:T(8,128)}), f32[2,256,256]{2,1,0:T(8,128)}) %all-reduce.6.cloned.1.call-update) | async-done | bytes 524304 | tf_op jit(solution)/shard_map/psum | solution.py:38
  573.2 1.3 multiply_reduce_fusion
  574.5 76.9 %all-reduce = (f32[]{:T(128)}, f32[]{:T(128)}) all-reduce(f32[]{:T(128)} %get-tuple-element.7, f32[]{:T(128)} %get-tuple-element.6), channel_id=1, replica_groups=mesh['ops'=32,'sec'=8] {'ops','sec'}, use_global_device_ids=true, to_apply=%region_12.0 | all-reduce | flops 2 | bytes 16 | tf_op jit(solution)/shard_map/psum | solution.py:56
  654.1 0.6 add_divide_fusion
  (6 shorter events, 0.1 us)
Async XLA Ops:
  7.2 84.7 %copy-start = (bf16[4,2,256,256]{3,2,1,0:T(8,128)(2,1)S(1)}, bf16[4,2,256,256]{3,2,1,0:T(8,128)(2,1)}, u32[]{:S(2)}) copy-start(bf16[4,2,256,256]{3,2,1,0:T(8,128)(2,1)} %param.6) | copy-start | bytes 3145732
  7.2 84.6 %copy-start.4 = (s32[4,2]{0,1:T(2,128)S(1)}, s32[4,2]{0,1:T(2,128)}, u32[]{:S(2)}) copy-start(s32[4,2]{0,1:T(2,128)} %param.8) | copy-start | bytes 100
  7.2 196.4 %all-reduce.4.cloned.1.call-start = ((), (), s32[]{:S(2)}) async-start(), calls=%async_computation | async-start | bytes 1048576 | tf_op jit(solution)/shard_map/psum | solution.py:38
  91.8 195.3 %copy-start.1 = (f32[2,256,256]{2,1,0:T(8,128)S(1)}, f32[2,256,256]{2,1,0:T(8,128)}, u32[]{:S(2)}) copy-start(f32[2,256,256]{2,1,0:T(8,128)} %param.9) | copy-start | bytes 1572868
  91.8 195.3 %copy-start.2 = (f32[2,256,256]{2,1,0:T(8,128)S(1)}, f32[2,256,256]{2,1,0:T(8,128)}, u32[]{:S(2)}) copy-start(f32[2,256,256]{2,1,0:T(8,128)} %param.10) | copy-start | bytes 1572868
  94.7 478.5 %all-reduce.6.cloned.1.call-start = ((), (), s32[]{:S(2)}) async-start(), calls=%async_computation.1 | async-start | bytes 1048576 | tf_op jit(solution)/shard_map/psum | solution.py:38
  288.3 74.6 %copy-start.3 = (bf16[2,256,8]{1,2,0:T(8,128)(2,1)S(1)}, bf16[2,256,8]{1,2,0:T(8,128)(2,1)}, u32[]{:S(2)}) copy-start(bf16[2,256,8]{1,2,0:T(8,128)(2,1)} %param.11) | copy-start | bytes 24580
Sparse Core Ops, SparseCore 0:
  94.8 108.7 all-reduce.3
  464.0 109.0 all-reduce.5
